TPU v7x, 512 devices: a whole 4x8x8 slice. The times are simulated.
512 devices in a mesh: angle: 16 (over y, core), tile: 32 (over x, z).
Axes of the slice: x: 4, y: 8, z: 8, core: 2. Of those that a mesh axis runs over, the one named last changes fastest.
Arguments:
- patches: bfloat16 [16, 256, 2, 128, 128], P('angle', 'tile'), may hold values from -6 to 6
- magnitudes: bfloat16 [16, 2048, 128, 128], P('angle', 'tile'), may hold values from 0.099609375 to 3
- probe: float32 [2, 128, 128], replicated, may hold values from -6 to 6
- owners: int32 [16, 256, 1], P('angle', 'tile'), may hold values from 0 to 31; in each aligned block of 8 rows (0 to 7, 8 to 15, ..., all dimensions but the last counted through in order) at most 2 rows name the same one
- scan_rows: int32 [16, 256], P('angle', 'tile'), may hold values from 0 to 384
- scan_cols: int32 [16, 256], P('angle', 'tile'), may hold values from 0 to 896
- slab_rows: int32 [32, 16], P('tile'), may hold values from 0 to 2, as said below
- angle_tan: float32 [16], replicated, may hold values from -0.4 to 0.4
- prior_in: bfloat16 [16, 1, 3, 3], replicated, may hold values from -2 to 2
- prior_out: bfloat16 [1, 16, 3, 3], replicated, may hold values from -0.5 to 0.5
Outputs:
- volume: float32 [32, 32, 16, 1024], P('tile', 'angle')
Inputs may be any that keep to these rules, and one draw needn't show every extreme that they name: `owners`: in the patches of one device, no owner is named by more than 2, and in some devices one owner is named exactly 2 times. Each row of slab_rows sums to 16, and in every row some slab has exactly 2 rows.
All inputs are finite; a program needn't handle non-finite values.
Results may differ from a plain program's by a relative error of at most 0.022.
Values may be sent and summed in bfloat16 or wider, within the bound.
A program may use at most 64 MiB of HBM per device.

v0:
```python
import math
import jax
import jax.numpy as jnp
from jax import lax
from jax.sharding import PartitionSpec as P

H = 512
W = 1024
XW = 16


def dft_table(side):
    index = jnp.arange(side, dtype=jnp.int32)
    product = index[:, None] * index[None, :] % side
    phase = product.astype(jnp.float32) * (2.0 * math.pi / side)
    scale = 1.0 / math.sqrt(side)
    real = jnp.cos(phase) * scale
    imag = -jnp.sin(phase) * scale
    upper = jnp.concatenate([real, imag], axis=1)
    lower = jnp.concatenate([-imag, real], axis=1)
    return jnp.concatenate([upper, lower], axis=0).astype(jnp.bfloat16)


def correct_all(waves, measured, table):
    number = waves.shape[0]
    side = waves.shape[2]
    left = table.T
    joined = jnp.concatenate([waves[:, 0], waves[:, 1]], axis=2).reshape(number * side, 2 * side)
    half = jnp.dot(joined, table, preferred_element_type=jnp.float32).astype(jnp.bfloat16)
    half = half.reshape(number, side, 2 * side)
    stacked = jnp.concatenate([half[:, :, :side], half[:, :, side:]], axis=1)
    stacked = jnp.transpose(stacked, (1, 0, 2)).reshape(2 * side, number * side)
    spectrum = jnp.dot(left, stacked, preferred_element_type=jnp.float32).reshape(
        2 * side, number, side
    )
    real_part = spectrum[:side]
    imag_part = spectrum[side:]
    level = jnp.transpose(measured, (1, 0, 2)).astype(jnp.float32)
    factor = level / jnp.sqrt(real_part * real_part + imag_part * imag_part + 0.25)
    target = jnp.concatenate([real_part * factor, imag_part * factor], axis=2).astype(jnp.bfloat16)
    back = jnp.dot(
        target.reshape(side * number, 2 * side), left, preferred_element_type=jnp.float32
    )
    back = back.astype(jnp.bfloat16).reshape(side, number, 2 * side)
    stacked_back = jnp.concatenate([back[:, :, :side], back[:, :, side:]], axis=0).reshape(
        2 * side, number * side
    )
    result = jnp.dot(table, stacked_back, preferred_element_type=jnp.float32).reshape(
        2, side, number, side
    )
    return jnp.transpose(result, (2, 0, 1, 3)).astype(jnp.bfloat16)


def backproject(sino, angle_tan, width):
    count = sino.shape[1]
    offsets = jnp.arange(XW, dtype=jnp.float32) - (XW - 1) / 2.0
    spread_cols = int(0.2 * (XW - 1)) + 2
    shifts = jnp.arange(-spread_cols, spread_cols + 1, dtype=jnp.int32).astype(jnp.float32)

    def add_angle(total, item):
        rows, tangent = item
        shifted = offsets * tangent
        floor_shift = jnp.floor(shifted)
        fraction = shifted - floor_shift
        low_hit = (shifts[None, :] == floor_shift[:, None]).astype(jnp.float32)
        high_hit = (shifts[None, :] == floor_shift[:, None] + 1.0).astype(jnp.float32)
        weights = (1.0 - fraction)[:, None] * low_hit + fraction[:, None] * high_hit
        padded = jnp.pad(rows, ((0, 0), (spread_cols, spread_cols)))
        columns_stack = jnp.stack(
            [padded[:, step : step + width] for step in range(2 * spread_cols + 1)], axis=0
        )
        term = jnp.einsum("is,scj->cij", weights, columns_stack, precision=lax.Precision.HIGHEST)
        return (total + term, None)

    start = jnp.zeros((count, XW, width), jnp.float32)
    total, unused = lax.scan(add_angle, start, (sino, angle_tan))
    return total / sino.shape[0]


def prior(slices, prior_in, prior_out):
    numbers = ("NCHW", "OIHW", "NCHW")
    rounded = slices.astype(jnp.bfloat16)[:, None].astype(jnp.float32)
    hidden = lax.conv_general_dilated(
        rounded, prior_in.astype(jnp.float32), (1, 1), "SAME", dimension_numbers=numbers
    )
    hidden = jnp.maximum(hidden, 0.0).astype(jnp.bfloat16).astype(jnp.float32)
    extra = lax.conv_general_dilated(
        hidden, prior_out.astype(jnp.float32), (1, 1), "SAME", dimension_numbers=numbers
    )
    return slices + extra[:, 0]


def body(
    patches,
    magnitudes,
    probe,
    owners,
    scan_rows,
    scan_cols,
    slab_rows,
    angle_tan,
    prior_in,
    prior_out,
):
    tiles = lax.axis_size("tile")
    angles = lax.axis_size("angle")
    count = patches.shape[1]
    side = patches.shape[3]
    slots = magnitudes.shape[1]
    depth = slots // tiles
    table = dft_table(side)
    owner = owners[0, :, 0]
    member = (owner[:, None] == jnp.arange(tiles, dtype=jnp.int32)[None, :]).astype(jnp.int32)
    before = jnp.sum((jnp.cumsum(member, axis=0) - member) * member, axis=1)
    slot = owner * depth + before
    select = (jnp.arange(slots, dtype=jnp.int32)[:, None] == slot[None, :]).astype(jnp.bfloat16)
    waves = patches[0]
    packed = jnp.dot(select, waves.reshape(count, -1), preferred_element_type=jnp.float32).astype(
        jnp.bfloat16
    )
    arrived = lax.all_to_all(
        packed.reshape(tiles, depth, 2, side, side), "tile", split_axis=0, concat_axis=0, tiled=True
    )
    fixed = correct_all(arrived.reshape(slots, 2, side, side), magnitudes[0], table)
    returned = lax.all_to_all(
        fixed.reshape(tiles, depth, 2, side, side), "tile", split_axis=0, concat_axis=0, tiled=True
    )
    mine = jnp.dot(select.T, returned.reshape(slots, -1), preferred_element_type=jnp.float32)
    mine = mine.astype(jnp.bfloat16).reshape(count, 2, side, side)
    mine_float = mine.astype(jnp.float32)
    contrib = (probe[0] * mine_float[:, 1] - probe[1] * mine_float[:, 0]) * 0.25
    rows_here = scan_rows[0]
    cols_here = scan_cols[0]
    width = W

    def place(step, canvas):
        row = rows_here[step]
        col = cols_here[step]
        piece = lax.dynamic_slice(canvas, (row, col), (side, side)) + contrib[step]
        return lax.dynamic_update_slice(canvas, piece, (row, col))

    canvas = lax.fori_loop(0, count, place, jnp.zeros((H, width), jnp.float32))
    strip = lax.psum_scatter(
        canvas.astype(jnp.bfloat16), "tile", scatter_dimension=0, tiled=True
    ).astype(jnp.float32)
    strip_rows = strip.shape[0]
    rowcap = 2 * strip_rows // angles
    lengths = slab_rows[0]
    starts = jnp.cumsum(lengths) - lengths
    within = jnp.arange(rowcap, dtype=jnp.int32)
    index = jnp.clip(starts[:, None] + within[None, :], 0, strip_rows - 1)
    valid = (within[None, :] < lengths[:, None]).astype(jnp.float32)
    outgoing = strip[index] * valid[:, :, None]
    slabs = prior(
        backproject(
            lax.all_to_all(
                outgoing.astype(jnp.bfloat16), "angle", split_axis=0, concat_axis=0, tiled=True
            ).astype(outgoing.dtype),
            angle_tan,
            width,
        ),
        prior_in,
        prior_out,
    )
    return slabs[None]


def solution(mesh):
    placed = (
        P("angle", "tile", None, None, None),
        P("angle", "tile", None, None),
        P(),
        P("angle", "tile", None),
        P("angle", "tile"),
        P("angle", "tile"),
        P("tile", None),
        P(),
        P(),
        P(),
    )
    return jax.shard_map(
        body, mesh=mesh, in_specs=placed, out_specs=P("tile", "angle", None, None), check_vma=False
    )
```

profile of v0, /device:TPU:1, one launch (start us, length us, event | category | flops | bytes accessed | tf_op | source)
XLA Modules:
  0.0 744.7 jit_solution(15535922218430683627)
XLA Ops:
  11.3 3.1 copy.119
  14.4 14.0 %all-to-all-start = ((bf16[32,2,2,128,128]{4,3,2,1,0:T(8,128)(2,1)}), bf16[32,2,2,128,128]{4,3,2,1,0:T(8,128)(2,1)}, u32[]{:S(2)}, u32[]{:S(2)}) async-start(bf16[32,2,2,128,128]{4,3,2,1,0:T(8,128)(2,1)} %bitcast.193), calls=%async_computation | async-start | bytes 8388608 | tf_op jit(solution)/shard_map/all_to_all | solution.py:121
  29.0 91.9 %all-to-all-done = bf16[32,2,2,128,128]{4,3,2,1,0:T(8,128)(2,1)} async-done(((bf16[32,2,2,128,128]{4,3,2,1,0:T(8,128)(2,1)}), bf16[32,2,2,128,128]{4,3,2,1,0:T(8,128)(2,1)}, u32[]{:S(2)}, u32[]{:S(2)}) %all-to-all-start) | async-done | bytes 4194336 | tf_op jit(solution)/shard_map/all_to_all | solution.py:121
  121.0 2.7 fusion.82
  125.0 2.5 fusion.81
  127.5 4.1 copy.115
  131.6 2.9 copy.116
  134.5 2.9 pad_maximum_fusion
  141.9 6.8 fusion.35
  151.3 2.3 pad_maximum_fusion.1
  153.6 7.0 copy.112
  160.6 3.5 fusion.44
  164.1 2.3 copy.100
  166.4 9.7 %all-to-all-start.1 = ((bf16[32,2,2,128,128]{4,3,2,1,0:T(8,128)(2,1)}), bf16[32,2,2,128,128]{4,3,2,1,0:T(8,128)(2,1)}, u32[]{:S(2)}, u32[]{:S(2)}) async-start(bf16[32,2,2,128,128]{4,3,2,1,0:T(8,128)(2,1)} %copy.100), calls=%async_computation.1 | async-start | bytes 8388608 | tf_op jit(solution)/shard_map/all_to_all | solution.py:125
  176.2 92.5 %all-to-all-done.1 = bf16[32,2,2,128,128]{4,3,2,1,0:T(8,128)(2,1)} async-done(((bf16[32,2,2,128,128]{4,3,2,1,0:T(8,128)(2,1)}), bf16[32,2,2,128,128]{4,3,2,1,0:T(8,128)(2,1)}, u32[]{:S(2)}, u32[]{:S(2)}) %all-to-all-start.1) | async-done | bytes 4194336 | tf_op jit(solution)/shard_map/all_to_all | solution.py:125
  268.7 7.4 reshape.187
  276.1 2.9 convolution_convert_fusion.1
  279.6 60.7 %while.27 = (s32[]{:T(128)}, f32[512,1024]{1,0:T(8,128)S(1)}, s32[8]{0:T(128)S(1)}, s32[8]{0:T(128)S(1)}, f32[8,128,128]{2,1,0:T(8,128)S(1)}, /*index=5*/s32[]{:T(128)}, s32[]{:T(128)}, s32[]{:T(128)}, s32[]{:T(128)}) while((s32[]{:T(128)}, f32[512,1024]{1,0:T(8,128)S(1)}, s32[8]{0:T(128)S(1)}, s32[8]{0:T(128)S(1)}, ...), condition=%wide.region_3.4_spmd, body=%wide.region_2.3_spmd.sunk | while | flops 16392 | bytes 327881 | solution.py:142
  342.0 216.4 %reduce-scatter.2.cloned.1.call-done = bf16[16,1024]{1,0:T(8,128)(2,1)} async-done(((bf16[512,1024]{1,0:T(8,128)(2,1)}), bf16[16,1024]{1,0:T(8,128)(2,1)}) %reduce-scatter.2.cloned.1.call-update) | async-done | bytes 32784 | tf_op jit(solution)/shard_map/reduce_scatter | solution.py:143
  560.6 12.6 %all-to-all-start.2 = ((bf16[16,2,1024]{2,1,0:T(2,128)(2,1)}), bf16[16,2,1024]{2,1,0:T(2,128)(2,1)S(1)}, u32[]{:S(2)}, u32[]{:S(2)}) async-start(bf16[16,2,1024]{2,1,0:T(2,128)(2,1)} %multiply_convert_fusion), calls=%async_computation.3 | async-start | bytes 131072 | tf_op jit(solution)/shard_map/all_to_all | solution.py:156
  573.2 7.8 %all-to-all-done.2 = bf16[16,2,1024]{2,1,0:T(2,128)(2,1)S(1)} async-done(((bf16[16,2,1024]{2,1,0:T(2,128)(2,1)}), bf16[16,2,1024]{2,1,0:T(2,128)(2,1)S(1)}, u32[]{:S(2)}, u32[]{:S(2)}) %all-to-all-start.2) | async-done | bytes 65568 | tf_op jit(solution)/shard_map/all_to_all | solution.py:156
  581.1 46.0 %while.28 = (s32[]{:T(128)}, f32[2,16,1024]{2,1,0:T(8,128)S(1)}, f32[16,2,1024]{2,1,0:T(2,128)S(1)}, f32[16]{0:T(128)S(1)}, s32[]{:T(128)}, /*index=5*/s32[]{:T(128)}) while((s32[]{:T(128)}, f32[2,16,1024]{2,1,0:T(8,128)S(1)}, f32[16,2,1024]{2,1,0:T(2,128)S(1)}, f32[16]{0:T(128)S(1)}, s32[]{:T(128)}, ...), condition=%wide.region_7.8_spmd.clone.clone, body=%wide.region_6.7_spmd.clone.clone.sunk | while | flops 4391977 | bytes 844483 | solution.py:76
  628.9 8.3 %fusion.28 = bf16[16,2,8,129,16]{4,2,1,3,0:T(8,128)(2,1)S(1)} fusion(pred[16,129]{0,1:T(8,128)(4,1)S(1)} %copy-done.9, bf16[1,16,16,131]{2,0,3,1:T(2,128)(2,1)S(1)} %copy.106, bf16[16,1,3,3]{0,3,2,1:T(4,128)(2,1)S(1)} %copy-done), kind=kOutput, calls=%fused_computation.50 | convolution fusion | flops 11228160 | bytes 1126192 | tf_op jit(solution)/shard_map/conv_general_dilated | solution.py:83
  637.3 98.4 %fusion.25 = f32[16,16,129,1]{1,3,2,0:T(1,128)S(1)} fusion(bf16[16,2,7,1,16]{4,2,1,3,0:T(8,128)(2,1)S(1)} %get-tuple-element.258, bf16[16,2,7,1,16]{4,2,1,3,0:T(8,128)(2,1)S(1)} %get-tuple-element.257, bf16[16,2,8,129,16]{4,2,1,3,0:T(8,128)(2,1)S(1)} %fusion.28, bf16[1,16,3,3]{1,3,2,0:T(4,128)(2,1)S(1)} %copy-done.5), kind=kOutput, calls=%fused_computation.48 | convolution fusion | flops 14480384 | bytes 1203488 | tf_op jit(solution)/shard_map/conv_general_dilated | solution.py:87
  (436 shorter events, 92.8 us)
Async XLA Ops:
  6.5 622.3 %copy-start = (bf16[16,1,3,3]{0,3,2,1:T(4,128)(2,1)S(1)}, bf16[16,1,3,3]{0,3,2,1:T(4,128)(2,1)}, u32[]{:S(2)}) copy-start(bf16[16,1,3,3]{0,3,2,1:T(4,128)(2,1)} %param.22) | copy-start | bytes 868
  14.4 106.5 %all-to-all-start = ((bf16[32,2,2,128,128]{4,3,2,1,0:T(8,128)(2,1)}), bf16[32,2,2,128,128]{4,3,2,1,0:T(8,128)(2,1)}, u32[]{:S(2)}, u32[]{:S(2)}) async-start(bf16[32,2,2,128,128]{4,3,2,1,0:T(8,128)(2,1)} %bitcast.193), calls=%async_computation | async-start | bytes 8388608 | tf_op jit(solution)/shard_map/all_to_all | solution.py:121
  140.4 1.6 copy-start.2
  166.4 9.8 %copy-start.3 = (f32[2,128,128]{2,1,0:T(8,128)S(1)}, f32[2,128,128]{2,1,0:T(8,128)}, u32[]{:S(2)}) copy-start(f32[2,128,128]{2,1,0:T(8,128)} %param.16) | copy-start | bytes 393220
  166.4 102.4 %all-to-all-start.1 = ((bf16[32,2,2,128,128]{4,3,2,1,0:T(8,128)(2,1)}), bf16[32,2,2,128,128]{4,3,2,1,0:T(8,128)(2,1)}, u32[]{:S(2)}, u32[]{:S(2)}) async-start(bf16[32,2,2,128,128]{4,3,2,1,0:T(8,128)(2,1)} %copy.100), calls=%async_computation.1 | async-start | bytes 8388608 | tf_op jit(solution)/shard_map/all_to_all | solution.py:125
  176.1 382.3 %reduce-scatter.2.cloned.1.call-start = ((), (), s32[]{:S(2)}) async-start(), calls=%async_computation.4 | async-start | bytes 1081344 | tf_op jit(solution)/shard_map/reduce_scatter | solution.py:143
  276.1 3.5 copy-start.6
  276.1 3.5 copy-start.7
  279.3 62.2 %copy-start.4 = (s32[1,16]{1,0:T(1,128)S(1)}, s32[1,16]{1,0:T(1,128)}, u32[]{:S(2)}) copy-start(s32[1,16]{1,0:T(1,128)} %param.20) | copy-start | bytes 196
  279.6 301.5 %copy-start.8 = (f32[16]{0:T(128)S(1)}, f32[16]{0:T(128)}, u32[]{:S(2)}) copy-start(f32[16]{0:T(128)} %param.21) | copy-start | bytes 196
  559.8 69.1 %copy-start.9 = (pred[16,129]{0,1:T(8,128)(4,1)S(1)}, pred[16,129]{0,1:T(8,128)(4,1)}, u32[]{:S(2)}) copy-start(pred[16,129]{0,1:T(8,128)(4,1)} %constant.130) | copy-start | bytes 6196
  560.6 20.4 %all-to-all-start.2 = ((bf16[16,2,1024]{2,1,0:T(2,128)(2,1)}), bf16[16,2,1024]{2,1,0:T(2,128)(2,1)S(1)}, u32[]{:S(2)}, u32[]{:S(2)}) async-start(bf16[16,2,1024]{2,1,0:T(2,128)(2,1)} %multiply_convert_fusion), calls=%async_computation.3 | async-start | bytes 131072 | tf_op jit(solution)/shard_map/all_to_all | solution.py:156
  628.8 8.4 %copy-start.5 = (bf16[1,16,3,3]{1,3,2,0:T(4,128)(2,1)S(1)}, bf16[1,16,3,3]{1,3,2,0:T(4,128)(2,1)}, u32[]{:S(2)}) copy-start(bf16[1,16,3,3]{1,3,2,0:T(4,128)(2,1)} %param.23) | copy-start | bytes 868
  637.2 100.4 %copy-start.1 = (bf16[16,1,3,3]{0,3,2,1:T(4,128)(2,1)S(1)}, bf16[16,1,3,3]{0,3,2,1:T(4,128)(2,1)}, u32[]{:S(2)}) copy-start(bf16[16,1,3,3]{0,3,2,1:T(4,128)(2,1)} %param.22) | copy-start | bytes 868
Sparse Core Ops, SparseCore 0:
  341.6 216.7 reduce-scatter.1
where the time goes:
time: 749 us; the launch traced here: 745 us
  waiting for transfers between devices  409 us (55%)
  matrix products  123 us (16%)
  local copies, waits for them, and re-layouts  86.2 us (12%)
  other arithmetic  40.3 us (5%)
  starting transfers between devices  36.4 us (5%)
  loops' own time  35.7 us (5%)
  between operations  14 us (2%)
    reduce_scatter x1, waiting for transfers between devices, body(): lax.psum_scatter(canvas.astype(jnp.bfloat16), 'tile', scatter_dimension=0...  216 us
    conv_general_dilated x1, matrix products, prior(): lax.conv_general_dilated(hidden, prior_out.astype(jnp.float32), (1, 1), '...  98.4 us
    all_to_all x1, waiting for transfers between devices, body(): lax.all_to_all(fixed.reshape(tiles, depth, 2, side, side), 'tile', split_...  92.5 us
    all_to_all x1, waiting for transfers between devices, body(): lax.all_to_all(packed.reshape(tiles, depth, 2, side, side), 'tile', split...  91.9 us
    another operation x1, loops' own time, body(): canvas = lax.fori_loop(0, count, place, jnp.zeros((H, width), jnp.float32))  33.3 us
    dynamic_update_slice x8, local copies, waits for them, and re-layouts, place(): return lax.dynamic_update_slice(canvas, piece, (row, col))  16 us
  transfers between devices with their start and end apart: 4, of which 4 were waited for; matrix products, arithmetic and copies ran while one was open for 0% of the time, Pallas kernels for 0%

commit v1 on v0

--- a/solution.py
+++ b/solution.py
@@ -7,6 +7,22 @@
 H = 512
 W = 1024
 XW = 16
+
+
+def exchange_in_pairs(array, axis, split, join):
+    ways, here = (lax.axis_size(axis), lax.axis_index(axis))
+    width = array.shape[split] // ways
+    lengths = list(array.shape)
+    lengths[split] = width
+    height = lengths[join]
+    lengths[join] = height * ways
+    full = jnp.zeros(lengths, array.dtype)
+    for mask in range(ways):
+        part = lax.dynamic_slice_in_dim(array, (here ^ mask) * width, width, axis=split)
+        if mask:
+            part = lax.ppermute(part, axis, [(d, d ^ mask) for d in range(ways)])
+        full = lax.dynamic_update_slice_in_dim(full, part, (here ^ mask) * height, axis=join)
+    return full
 
 
 def dft_table(side):
@@ -153,9 +169,7 @@
     outgoing = strip[index] * valid[:, :, None]
     slabs = prior(
         backproject(
-            lax.all_to_all(
-                outgoing.astype(jnp.bfloat16), "angle", split_axis=0, concat_axis=0, tiled=True
-            ).astype(outgoing.dtype),
+            exchange_in_pairs(outgoing.astype(jnp.bfloat16), "angle", 0, 0).astype(outgoing.dtype),
             angle_tan,
             width,
         ),

time: 749 us -> 797 us (1.064)
  starting transfers between devices: 36.4 us -> 83.3 us
  matrix products: 123 us -> 139 us
    ppermute x0 -> x15, starting transfers between devices: none -> 59.5 us  [exchange_in_pairs(): part = lax.ppermute(part, axis, [(d, d ^ mask) for d in range(ways)])]
    conv_general_dilated x1, matrix products: 98.4 us -> 114 us  [prior(): lax.conv_general_dilated(hidden, prior_out.astype(jnp.float32), (1, 1), '...]
    all_to_all x1 -> x0, starting transfers between devices: 12.6 us -> none  [body(): lax.all_to_all(outgoing.astype(jnp.bfloat16), 'angle', split_axis=0, conc...]
  transfers between devices with their start and end apart: 4 -> 18, of which waited for: 4 -> 4; matrix products, arithmetic and copies ran while one was open for 0% -> 0% of each run, Pallas kernels for 0% -> 0%
where the time goes in v1:
time: 797 us; the launch traced here: 793 us
  waiting for transfers between devices  404 us (51%)
  matrix products  139 us (17%)
  local copies, waits for them, and re-layouts  86.1 us (11%)
  starting transfers between devices  83.3 us (10%)
  other arithmetic  36.9 us (5%)
  loops' own time  29.9 us (4%)
  between operations  14.5 us (2%)
    reduce_scatter x1, waiting for transfers between devices, body(): lax.psum_scatter(canvas.astype(jnp.bfloat16), 'tile', scatter_dimension=0...  216 us
    conv_general_dilated x1, matrix products, prior(): lax.conv_general_dilated(hidden, prior_out.astype(jnp.float32), (1, 1), '...  114 us
    all_to_all x1, waiting for transfers between devices, body(): lax.all_to_all(fixed.reshape(tiles, depth, 2, side, side), 'tile', split_...  92.6 us
    all_to_all x1, waiting for transfers between devices, body(): lax.all_to_all(packed.reshape(tiles, depth, 2, side, side), 'tile', split...  91.9 us
    ppermute x15, starting transfers between devices, exchange_in_pairs(): part = lax.ppermute(part, axis, [(d, d ^ mask) for d in range(ways)])  59.5 us
    another operation x1, loops' own time, body(): canvas = lax.fori_loop(0, count, place, jnp.zeros((H, width), jnp.float32))  27.6 us
    dynamic_update_slice x8, local copies, waits for them, and re-layouts, place(): return lax.dynamic_update_slice(canvas, piece, (row, col))  16 us
  transfers between devices with their start and end apart: 18, of which 4 were waited for; matrix products, arithmetic and copies ran while one was open for 0% of the time, Pallas kernels for 0%

profile of v1, /device:TPU:1, one launch (start us, length us, event | category | flops | bytes accessed | tf_op | source)
XLA Modules:
  0.0 793.1 jit_solution(14614881016908329928)
XLA Ops:
  11.3 3.2 copy.118
  14.5 14.0 %all-to-all-start = ((bf16[32,2,2,128,128]{4,3,2,1,0:T(8,128)(2,1)}), bf16[32,2,2,128,128]{4,3,2,1,0:T(8,128)(2,1)}, u32[]{:S(2)}, u32[]{:S(2)}) async-start(bf16[32,2,2,128,128]{4,3,2,1,0:T(8,128)(2,1)} %bitcast.193), calls=%async_computation | async-start | bytes 8388608 | tf_op jit(solution)/shard_map/all_to_all | solution.py:137
  29.1 91.9 %all-to-all-done = bf16[32,2,2,128,128]{4,3,2,1,0:T(8,128)(2,1)} async-done(((bf16[32,2,2,128,128]{4,3,2,1,0:T(8,128)(2,1)}), bf16[32,2,2,128,128]{4,3,2,1,0:T(8,128)(2,1)}, u32[]{:S(2)}, u32[]{:S(2)}) %all-to-all-start) | async-done | bytes 4194336 | tf_op jit(solution)/shard_map/all_to_all | solution.py:137
  127.5 4.1 copy.114
  141.9 6.7 fusion.35
  153.5 7.0 copy.112
  160.5 3.5 fusion.44
  166.3 9.7 %all-to-all-start.1 = ((bf16[32,2,2,128,128]{4,3,2,1,0:T(8,128)(2,1)}), bf16[32,2,2,128,128]{4,3,2,1,0:T(8,128)(2,1)}, u32[]{:S(2)}, u32[]{:S(2)}) async-start(bf16[32,2,2,128,128]{4,3,2,1,0:T(8,128)(2,1)} %copy.100), calls=%async_computation.1 | async-start | bytes 8388608 | tf_op jit(solution)/shard_map/all_to_all | solution.py:141
  176.1 92.6 %all-to-all-done.1 = bf16[32,2,2,128,128]{4,3,2,1,0:T(8,128)(2,1)} async-done(((bf16[32,2,2,128,128]{4,3,2,1,0:T(8,128)(2,1)}), bf16[32,2,2,128,128]{4,3,2,1,0:T(8,128)(2,1)}, u32[]{:S(2)}, u32[]{:S(2)}) %all-to-all-start.1) | async-done | bytes 4194336 | tf_op jit(solution)/shard_map/all_to_all | solution.py:141
  268.7 7.3 reshape.187
  279.6 53.6 %while.27 = (s32[]{:T(128)}, f32[512,1024]{1,0:T(8,128)S(1)}, s32[8]{0:T(128)S(1)}, s32[8]{0:T(128)S(1)}, f32[8,128,128]{2,1,0:T(8,128)S(1)}, /*index=5*/s32[]{:T(128)}, s32[]{:T(128)}, s32[]{:T(128)}, s32[]{:T(128)}) while((s32[]{:T(128)}, f32[512,1024]{1,0:T(8,128)S(1)}, s32[8]{0:T(128)S(1)}, s32[8]{0:T(128)S(1)}, ...), condition=%wide.region_3.4_spmd, body=%wide.region_2.3_spmd.sunk | while | flops 16392 | bytes 327881 | solution.py:158
  335.0 216.3 %reduce-scatter.2.cloned.1.call-done = bf16[16,1024]{1,0:T(8,128)(2,1)} async-done(((bf16[512,1024]{1,0:T(8,128)(2,1)}), bf16[16,1024]{1,0:T(8,128)(2,1)}) %reduce-scatter.2.cloned.1.call-update) | async-done | bytes 32784 | tf_op jit(solution)/shard_map/reduce_scatter | solution.py:159
  553.0 7.8 collective-permute-start
  566.3 4.1 collective-permute-start.3
  572.9 5.0 collective-permute-start.5
  580.2 7.2 collective-permute-start.7
  589.8 4.5 collective-permute-start.9
  594.3 4.0 collective-permute-start.10
  598.3 3.6 collective-permute-start.11
  601.9 4.2 collective-permute-start.12
  606.1 4.6 collective-permute-start.13
  617.0 43.0 %while.28 = (s32[]{:T(128)}, f32[2,16,1024]{2,1,0:T(8,128)S(1)}, f32[16,2,1024]{2,0,1:T(8,128)S(1)}, f32[16]{0:T(128)S(1)}, s32[]{:T(128)}, /*index=5*/s32[]{:T(128)}) while((s32[]{:T(128)}, f32[2,16,1024]{2,1,0:T(8,128)S(1)}, f32[16,2,1024]{2,0,1:T(8,128)S(1)}, f32[16]{0:T(128)S(1)}, s32[]{:T(128)}, ...), condition=%wide.region_7.8_spmd.clone.clone, body=%wide.region_6.7_spmd.clone.clone.sunk | while | flops 4391977 | bytes 828095 | solution.py:92
  661.8 8.3 %fusion.28 = bf16[16,2,8,129,16]{4,2,1,3,0:T(8,128)(2,1)S(1)} fusion(pred[16,129]{0,1:T(8,128)(4,1)S(1)} %copy-done.9, bf16[1,16,16,131]{2,0,3,1:T(2,128)(2,1)S(1)} %copy.106, bf16[16,1,3,3]{0,3,2,1:T(4,128)(2,1)S(1)} %copy-done), kind=kOutput, calls=%fused_computation.51 | convolution fusion | flops 11228160 | bytes 1126192 | tf_op jit(solution)/shard_map/conv_general_dilated | solution.py:99
  670.2 113.9 %fusion.25 = f32[16,16,129,1]{1,3,2,0:T(1,128)S(1)} fusion(bf16[16,2,7,1,16]{4,2,1,3,0:T(8,128)(2,1)S(1)} %get-tuple-element.250, bf16[16,2,7,1,16]{4,2,1,3,0:T(8,128)(2,1)S(1)} %get-tuple-element.249, bf16[16,2,8,129,16]{4,2,1,3,0:T(8,128)(2,1)S(1)} %fusion.28, bf16[1,16,3,3]{1,3,2,0:T(4,128)(2,1)S(1)} %copy-done.5), kind=kOutput, calls=%fused_computation.49 | convolution fusion | flops 14480384 | bytes 1203488 | tf_op jit(solution)/shard_map/conv_general_dilated | solution.py:103
  (466 shorter events, 125.4 us)
Async XLA Ops:
  6.5 655.3 %copy-start = (bf16[16,1,3,3]{0,3,2,1:T(4,128)(2,1)S(1)}, bf16[16,1,3,3]{0,3,2,1:T(4,128)(2,1)}, u32[]{:S(2)}) copy-start(bf16[16,1,3,3]{0,3,2,1:T(4,128)(2,1)} %param.22) | copy-start | bytes 868
  14.5 106.5 %all-to-all-start = ((bf16[32,2,2,128,128]{4,3,2,1,0:T(8,128)(2,1)}), bf16[32,2,2,128,128]{4,3,2,1,0:T(8,128)(2,1)}, u32[]{:S(2)}, u32[]{:S(2)}) async-start(bf16[32,2,2,128,128]{4,3,2,1,0:T(8,128)(2,1)} %bitcast.193), calls=%async_computation | async-start | bytes 8388608 | tf_op jit(solution)/shard_map/all_to_all | solution.py:137
  166.3 9.8 %copy-start.3 = (f32[2,128,128]{2,1,0:T(8,128)S(1)}, f32[2,128,128]{2,1,0:T(8,128)}, u32[]{:S(2)}) copy-start(f32[2,128,128]{2,1,0:T(8,128)} %param.16) | copy-start | bytes 393220
  166.3 102.4 %all-to-all-start.1 = ((bf16[32,2,2,128,128]{4,3,2,1,0:T(8,128)(2,1)}), bf16[32,2,2,128,128]{4,3,2,1,0:T(8,128)(2,1)}, u32[]{:S(2)}, u32[]{:S(2)}) async-start(bf16[32,2,2,128,128]{4,3,2,1,0:T(8,128)(2,1)} %copy.100), calls=%async_computation.1 | async-start | bytes 8388608 | tf_op jit(solution)/shard_map/all_to_all | solution.py:141
  176.1 375.2 %reduce-scatter.2.cloned.1.call-start = ((), (), s32[]{:S(2)}) async-start(), calls=%async_computation.3 | async-start | bytes 1081344 | tf_op jit(solution)/shard_map/reduce_scatter | solution.py:159
  279.3 55.1 %copy-start.4 = (s32[1,16]{1,0:T(1,128)S(1)}, s32[1,16]{1,0:T(1,128)}, u32[]{:S(2)}) copy-start(s32[1,16]{1,0:T(1,128)} %param.20) | copy-start | bytes 196
  279.6 337.4 %copy-start.8 = (f32[16]{0:T(128)S(1)}, f32[16]{0:T(128)}, u32[]{:S(2)}) copy-start(f32[16]{0:T(128)} %param.21) | copy-start | bytes 196
  552.6 109.2 %copy-start.9 = (pred[16,129]{0,1:T(8,128)(4,1)S(1)}, pred[16,129]{0,1:T(8,128)(4,1)}, u32[]{:S(2)}) copy-start(pred[16,129]{0,1:T(8,128)(4,1)} %constant.166) | copy-start | bytes 6196
  553.0 19.8 %collective-permute-start = (bf16[1,2,1024]{2,0,1:T(2,128)(2,1)S(1)}, bf16[1,2,1024]{2,0,1:T(2,128)(2,1)S(1)}, u32[]{:S(2)}, u32[]{:S(2)}) collective-permute-start(bf16[1,2,1024]{2,0,1:T(2,128)(2,1)S(1)} %get-tuple-element.277), channel_id=1, source_target_pairs={{0,32},{32,0},{64,96},{96,64},{128,160},{160,128},{192,224},{224,1... | collective-permute-start | bytes 12296 | tf_op jit(solution)/shard_map/ppermute | solution.py:23
  560.8 17.0 %collective-permute-start.1 = (bf16[1,2,1024]{2,0,1:T(2,128)(2,1)S(1)}, bf16[1,2,1024]{2,0,1:T(2,128)(2,1)S(1)}, u32[]{:S(2)}, u32[]{:S(2)}) collective-permute-start(bf16[1,2,1024]{2,0,1:T(2,128)(2,1)S(1)} %get-tuple-element.276), channel_id=1, source_target_pairs={{0,64},{32,96},{64,0},{96,32},{128,192},{160,224},{192,128},{224,1... | collective-permute-start | bytes 12296 | tf_op jit(solution)/shard_map/ppermute | solution.py:23
  564.0 16.2 %collective-permute-start.2 = (bf16[1,2,1024]{2,0,1:T(2,128)(2,1)S(1)}, bf16[1,2,1024]{2,0,1:T(2,128)(2,1)S(1)}, u32[]{:S(2)}, u32[]{:S(2)}) collective-permute-start(bf16[1,2,1024]{2,0,1:T(2,128)(2,1)S(1)} %get-tuple-element.275), channel_id=1, source_target_pairs={{0,96},{32,64},{64,32},{96,0},{128,224},{160,192},{192,160},{224,1... | collective-permute-start | bytes 12296 | tf_op jit(solution)/shard_map/ppermute | solution.py:23
  566.3 21.1 %collective-permute-start.3 = (bf16[1,2,1024]{2,0,1:T(2,128)(2,1)S(1)}, bf16[1,2,1024]{2,0,1:T(2,128)(2,1)S(1)}, u32[]{:S(2)}, u32[]{:S(2)}) collective-permute-start(bf16[1,2,1024]{2,0,1:T(2,128)(2,1)S(1)} %get-tuple-element.274), channel_id=1, source_target_pairs={{0,128},{32,160},{64,192},{96,224},{128,0},{160,32},{192,64},{224,... | collective-permute-start | bytes 12296 | tf_op jit(solution)/shard_map/ppermute | solution.py:23
  570.4 19.4 %collective-permute-start.4 = (bf16[1,2,1024]{2,0,1:T(2,128)(2,1)S(1)}, bf16[1,2,1024]{2,0,1:T(2,128)(2,1)S(1)}, u32[]{:S(2)}, u32[]{:S(2)}) collective-permute-start(bf16[1,2,1024]{2,0,1:T(2,128)(2,1)S(1)} %get-tuple-element.273), channel_id=1, source_target_pairs={{0,160},{32,128},{64,224},{96,192},{128,32},{160,0},{192,96},{224,... | collective-permute-start | bytes 12296 | tf_op jit(solution)/shard_map/ppermute | solution.py:23
  572.9 21.4 %collective-permute-start.5 = (bf16[1,2,1024]{2,0,1:T(2,128)(2,1)S(1)}, bf16[1,2,1024]{2,0,1:T(2,128)(2,1)S(1)}, u32[]{:S(2)}, u32[]{:S(2)}) collective-permute-start(bf16[1,2,1024]{2,0,1:T(2,128)(2,1)S(1)} %get-tuple-element.272), channel_id=1, source_target_pairs={{0,192},{32,224},{64,128},{96,160},{128,64},{160,96},{192,0},{224,... | collective-permute-start | bytes 12296 | tf_op jit(solution)/shard_map/ppermute | solution.py:23
  577.9 20.4 %collective-permute-start.6 = (bf16[1,2,1024]{2,0,1:T(2,128)(2,1)S(1)}, bf16[1,2,1024]{2,0,1:T(2,128)(2,1)S(1)}, u32[]{:S(2)}, u32[]{:S(2)}) collective-permute-start(bf16[1,2,1024]{2,0,1:T(2,128)(2,1)S(1)} %get-tuple-element.271), channel_id=1, source_target_pairs={{0,224},{32,192},{64,160},{96,128},{128,96},{160,64},{192,32},{224... | collective-permute-start | bytes 12296 | tf_op jit(solution)/shard_map/ppermute | solution.py:23
  580.2 21.7 %collective-permute-start.7 = (bf16[1,2,1024]{2,0,1:T(2,128)(2,1)S(1)}, bf16[1,2,1024]{2,0,1:T(2,128)(2,1)S(1)}, u32[]{:S(2)}, u32[]{:S(2)}) collective-permute-start(bf16[1,2,1024]{2,0,1:T(2,128)(2,1)S(1)} %get-tuple-element.270), channel_id=1, source_target_pairs={{0,256},{32,288},{64,320},{96,352},{128,384},{160,416},{192,448},{... | collective-permute-start | bytes 12296 | tf_op jit(solution)/shard_map/ppermute | solution.py:23
  587.3 18.7 %collective-permute-start.8 = (bf16[1,2,1024]{2,0,1:T(2,128)(2,1)S(1)}, bf16[1,2,1024]{2,0,1:T(2,128)(2,1)S(1)}, u32[]{:S(2)}, u32[]{:S(2)}) collective-permute-start(bf16[1,2,1024]{2,0,1:T(2,128)(2,1)S(1)} %get-tuple-element.269), channel_id=1, source_target_pairs={{0,288},{32,256},{64,352},{96,320},{128,416},{160,384},{192,480},{... | collective-permute-start | bytes 12296 | tf_op jit(solution)/shard_map/ppermute | solution.py:23
  589.8 20.9 %collective-permute-start.9 = (bf16[1,2,1024]{2,0,1:T(2,128)(2,1)S(1)}, bf16[1,2,1024]{2,0,1:T(2,128)(2,1)S(1)}, u32[]{:S(2)}, u32[]{:S(2)}) collective-permute-start(bf16[1,2,1024]{2,0,1:T(2,128)(2,1)S(1)} %get-tuple-element.268), channel_id=1, source_target_pairs={{0,320},{32,352},{64,256},{96,288},{128,448},{160,480},{192,384},{... | collective-permute-start | bytes 12296 | tf_op jit(solution)/shard_map/ppermute | solution.py:23
  594.3 19.5 %collective-permute-start.10 = (bf16[1,2,1024]{2,0,1:T(2,128)(2,1)S(1)}, bf16[1,2,1024]{2,0,1:T(2,128)(2,1)S(1)}, u32[]{:S(2)}, u32[]{:S(2)}) collective-permute-start(bf16[1,2,1024]{2,0,1:T(2,128)(2,1)S(1)} %get-tuple-element.267), channel_id=1, source_target_pairs={{0,352},{32,320},{64,288},{96,256},{128,480},{160,448},{192,416},{... | collective-permute-start | bytes 12296 | tf_op jit(solution)/shard_map/ppermute | solution.py:23
  598.3 15.6 %collective-permute-start.11 = (bf16[1,2,1024]{2,0,1:T(2,128)(2,1)S(1)}, bf16[1,2,1024]{2,0,1:T(2,128)(2,1)S(1)}, u32[]{:S(2)}, u32[]{:S(2)}) collective-permute-start(bf16[1,2,1024]{2,0,1:T(2,128)(2,1)S(1)} %get-tuple-element.266), channel_id=1, source_target_pairs={{0,384},{32,416},{64,448},{96,480},{128,256},{160,288},{192,320},{... | collective-permute-start | bytes 12296 | tf_op jit(solution)/shard_map/ppermute | solution.py:23
  601.9 12.1 %collective-permute-start.12 = (bf16[1,2,1024]{2,0,1:T(2,128)(2,1)S(1)}, bf16[1,2,1024]{2,0,1:T(2,128)(2,1)S(1)}, u32[]{:S(2)}, u32[]{:S(2)}) collective-permute-start(bf16[1,2,1024]{2,0,1:T(2,128)(2,1)S(1)} %get-tuple-element.265), channel_id=1, source_target_pairs={{0,416},{32,384},{64,480},{96,448},{128,288},{160,256},{192,352},{... | collective-permute-start | bytes 12296 | tf_op jit(solution)/shard_map/ppermute | solution.py:23
  606.1 8.0 %collective-permute-start.13 = (bf16[1,2,1024]{2,0,1:T(2,128)(2,1)S(1)}, bf16[1,2,1024]{2,0,1:T(2,128)(2,1)S(1)}, u32[]{:S(2)}, u32[]{:S(2)}) collective-permute-start(bf16[1,2,1024]{2,0,1:T(2,128)(2,1)S(1)} %get-tuple-element.264), channel_id=1, source_target_pairs={{0,448},{32,480},{64,384},{96,416},{128,320},{160,352},{192,256},{... | collective-permute-start | bytes 12296 | tf_op jit(solution)/shard_map/ppermute | solution.py:23
  610.7 6.2 collective-permute-start.14
  670.2 115.9 %copy-start.1 = (bf16[16,1,3,3]{0,3,2,1:T(4,128)(2,1)S(1)}, bf16[16,1,3,3]{0,3,2,1:T(4,128)(2,1)}, u32[]{:S(2)}) copy-start(bf16[16,1,3,3]{0,3,2,1:T(4,128)(2,1)} %param.22) | copy-start | bytes 868
  (4 other events, 17.0 us)
Sparse Core Ops, SparseCore 0:
  334.5 216.7 reduce-scatter.1
